TPU v7x, 32 devices: a whole 2x2x4 slice. The times are simulated.
32 devices in a mesh: groups: 2 (over x), dp: 8 (over z, y), tensor: 2 (over core).
Axes of the slice: x: 2, y: 2, z: 4, core: 2. Of those that a mesh axis runs over, the one named last changes fastest.
Arguments:
- step_hidden: bfloat16 [16, 32, 64, 4096], P('dp', 'groups', None, 'tensor'), parts along dimension 1, may hold values from -80 to 80
- prm_gain: float32 [4096], P('tensor'), may hold values from 0.1 to 1.9
- score_weight: float32 [4096], P('tensor'), may hold values from -0.09375 to 0.09375
- step_bounds: int32 [16, 32], P('dp', 'groups'), parts along dimension 1, may hold values from 0 to 63
- queries: bfloat16 [16, 32, 8192], P('dp', 'groups', 'tensor'), parts along dimension 1, may hold values from -16 to 16
- step_kv: bfloat16 [16, 32, 2, 64, 1024], P('dp', 'groups', None, None, 'tensor'), parts along dimension 1, may hold values from -4 to 4
- caches: bfloat16 [16, 32, 2, 128, 1024], P('dp', 'groups', None, None, 'tensor'), parts along dimension 1, may hold values from -4 to 4
- parents: int32 [16, 32, 1], P(None, 'groups'), parts along dimension 1, may hold values from 0 to 15; in each aligned block of 16 rows (0 to 15, 16 to 31, ..., all dimensions but the last counted through in order) at most 3 rows name the same one
- lengths: int32 [16, 32], P(None, 'groups'), parts along dimension 1, may hold values from 16 to 128
Outputs:
- attended: bfloat16 [16, 32, 8192], P('dp', 'groups', 'tensor'), parts along dimension 1
- prm_score: float32 [16, 32], P('dp', 'groups'), parts along dimension 1
There are 2 independent parts, one for each index of `groups`. A program takes and returns all parts, laid end to end along the dimension named above; an argument that names none is the same for every part. Nothing has to cross between parts.
Inputs may be any that keep to these rules, and one draw needn't show every extreme that they name: parents[b, p, 0] names the beam of problem p whose cache beam b continues. Among the problems of one beam b no beam is named by more than 3 problems, a bound that some block reaches.
All inputs are finite; a program needn't handle non-finite values.
Results may differ from a plain program's by a relative error of at most 0.001.
Values may be sent and summed in bfloat16 or wider, within the bound.
A program may use at most 192 MiB of HBM per device.

v0:
```python
import math

import jax
import jax.numpy as jnp
from jax import lax
from jax.sharding import PartitionSpec as P

HEAD = 128
D_PRM = 4096
PROB = 16
CTX = 128
STEP = 64
CAP = 3


def partial_attend(query, key_rows, value_rows, visible):
    dims = query.shape
    kv_heads = key_rows.shape[-1] // HEAD
    q_heads = dims[3] // HEAD
    query_heads = query.reshape(dims[0], dims[1], dims[2], kv_heads, q_heads // kv_heads, HEAD)
    key_heads = key_rows.reshape(
        key_rows.shape[0], key_rows.shape[1], key_rows.shape[2], kv_heads, HEAD
    )
    value_heads = value_rows.reshape(
        value_rows.shape[0], value_rows.shape[1], value_rows.shape[2], kv_heads, HEAD
    ).astype(jnp.float32)
    scores = jnp.einsum(
        "bprkgh,bptkh->bprkgt", query_heads, key_heads, preferred_element_type=jnp.float32
    ) * (1.0 / math.sqrt(HEAD))
    scores = jnp.where(visible[:, :, :, None, None, :], scores, -1e30)
    maxima = jnp.max(scores, axis=-1)
    weights = jnp.exp(scores - maxima[..., None])
    totals = jnp.sum(weights, axis=-1)
    numerators = jnp.einsum(
        "bprkgt,bptkh->bprkgh", weights, value_heads, precision=lax.Precision.HIGHEST
    )
    lead = (dims[0], dims[1], dims[2])
    return (
        maxima.reshape(lead + (q_heads,)),
        totals.reshape(lead + (q_heads,)),
        numerators.reshape(lead + (dims[3],)),
    )


def merge_parts(earlier_part, later_part):
    highest = jnp.maximum(earlier_part[0], later_part[0])
    scale_early = jnp.exp(earlier_part[0] - highest)
    scale_later = jnp.exp(later_part[0] - highest)
    totals = earlier_part[1] * scale_early + later_part[1] * scale_later
    lead = totals.shape
    heads = lead[-1]
    early_sum = earlier_part[2].reshape(lead + (earlier_part[2].shape[-1] // heads,))
    later_sum = later_part[2].reshape(lead + (later_part[2].shape[-1] // heads,))
    merged = (early_sum * scale_early[..., None] + later_sum * scale_later[..., None]) / totals[
        ..., None
    ]
    return merged.reshape(lead[:-1] + (earlier_part[2].shape[-1],))


def body(
    step_hidden, prm_gain, score_weight, step_bounds, queries, step_kv, caches, parents, lengths
):
    resident = step_hidden.shape[0]
    widened = step_hidden.astype(jnp.float32)
    squares = jnp.sum(widened * widened, axis=-1)
    products = jnp.sum(widened * (prm_gain * score_weight), axis=-1)
    squares, products = lax.psum((squares, products), "tensor")
    token_score = products / jnp.sqrt(squares / D_PRM + 1e-05)
    step_rows = jnp.arange(STEP, dtype=jnp.int32)
    step_live = step_rows[None, None, :] <= step_bounds[:, :, None]
    prm_score = jnp.max(jnp.where(step_live, token_score, -1e30), axis=-1)
    parent = parents[:, :, 0]
    problem = jnp.arange(PROB, dtype=jnp.int32)
    siblings = parent[:, :, None] == parent[:, None, :]
    earlier = problem[None, :] < problem[:, None]
    slot_all = jnp.sum(siblings & earlier[None, :, :], axis=-1)
    own_beams = lax.axis_index("dp") * resident + jnp.arange(resident, dtype=jnp.int32)
    own_parent = jnp.take(parent, own_beams, axis=0)
    own_slot = jnp.take(slot_all, own_beams, axis=0)
    slot_ids = jnp.arange(CAP, dtype=jnp.int32)
    resident_ids = jnp.arange(resident, dtype=jnp.int32)
    cache_rows = jnp.arange(CTX, dtype=jnp.int32)
    sender_match = (parent[:, None, None, :] == own_beams[None, :, None, None]) & (
        slot_all[:, None, None, :] == slot_ids[None, None, :, None]
    )
    sender_pick = jnp.sum(jnp.where(sender_match, problem, 0), axis=-1)
    query_rows = queries[:, :, None, :]
    own_part = partial_attend(
        query_rows, step_kv[:, :, 0], step_kv[:, :, 1], step_live[:, :, None, :]
    )
    outgoing = caches[resident_ids[None, :, None], sender_pick]
    arrived = lax.all_to_all(outgoing, "dp", split_axis=0, concat_axis=1, tiled=True)
    inherited = arrived[resident_ids[:, None], own_parent, own_slot]
    parent_len = lengths[own_parent, problem[None, :]]
    cache_live = (cache_rows[None, None, :] < parent_len[:, :, None])[:, :, None, :]
    cache_part = partial_attend(query_rows, inherited[:, :, 0], inherited[:, :, 1], cache_live)
    merged = merge_parts(cache_part, own_part)
    attended = merged.reshape(resident, PROB, queries.shape[-1]).astype(jnp.bfloat16)
    return (attended, prm_score)


def solution(mesh):
    in_specs = (
        P("dp", "groups", None, "tensor"),
        P("tensor"),
        P("tensor"),
        P("dp", "groups"),
        P("dp", "groups", "tensor"),
        P("dp", "groups", None, None, "tensor"),
        P("dp", "groups", None, None, "tensor"),
        P(None, "groups", None),
        P(None, "groups"),
    )
    out_specs = (P("dp", "groups", "tensor"), P("dp", "groups"))
    return jax.shard_map(body, mesh=mesh, in_specs=in_specs, out_specs=out_specs, check_vma=False)
```

profile of v0, /device:TPU:0, one launch (start us, length us, event | category | flops | bytes accessed | tf_op | source)
XLA Modules:
  0.0 635.6 jit_solution(11860904056210372157)
XLA Ops:
  0.7 1.2 convert_reduce_fusion
  1.9 0.8 broadcast_compare_fusion
  2.7 0.2 select_reduce_fusion
  2.9 0.1 copy.53
  3.0 0.1 reshape.249
  3.1 13.9 %gather_fusion = bf16[96,2,128,512]{3,2,1,0:T(8,128)(2,1)} fusion(bf16[2,16,2,128,512]{4,3,2,1,0:T(8,128)(2,1)} %param.17, s32[96]{0:T(128)S(1)} %reshape.249), kind=kCustom, calls=%fused_computation.2 | custom fusion | bytes 50332416 | tf_op jit(solution)/shard_map/gather | solution.py:91
  17.0 7.4 %all-to-all-start = ((bf16[16,2,3,2,128,512]{5,4,3,2,1,0:T(8,128)(2,1)}), bf16[16,2,3,2,128,512]{5,4,3,2,1,0:T(8,128)(2,1)}, u32[]{:S(2)}, u32[]{:S(2)}) async-start(bf16[16,2,3,2,128,512]{5,4,3,2,1,0:T(8,128)(2,1)} %bitcast.103), calls=%async_computation | async-start | bytes 50331648 | tf_op jit(solution)/shard_map/all_to_all | solution.py:92
  24.4 0.6 gather_fusion.4
  24.9 0.6 gather_fusion.3
  25.5 0.1 bitcast_or_fusion
  25.6 0.1 reshape.255
  25.7 0.1 reshape.261
  25.7 0.7 gather_fusion.2
  26.5 0.1 reshape.264
  26.6 3.9 fusion.44
  30.5 4.0 reshape_squeeze.14
  34.6 0.1 iota_compare_fusion.1
  34.6 2.9 fusion.45
  37.5 0.1 copy.61
  37.6 0.4 fusion.27
  38.1 0.1 copy.66
  38.1 2.1 reshape_squeeze.15
  40.2 3.4 fusion.6
  43.6 0.1 reshape_reshape.8
  43.7 6.3 fusion.1
  50.0 3.6 all-reduce
  53.6 0.7 select_reduce_fusion.1
  54.3 0.1 iota_compare_fusion.2
  54.4 514.2 %all-to-all-done = bf16[16,2,3,2,128,512]{5,4,3,2,1,0:T(8,128)(2,1)} async-done(((bf16[16,2,3,2,128,512]{5,4,3,2,1,0:T(8,128)(2,1)}), bf16[16,2,3,2,128,512]{5,4,3,2,1,0:T(8,128)(2,1)}, u32[]{:S(2)}, u32[]{:S(2)}) %all-to-all-start) | async-done | bytes 25165856 | tf_op jit(solution)/shard_map/all_to_all | solution.py:92
  568.6 20.7 %copy.54 = bf16[2,8,2,3,2,128,512]{6,5,4,3,2,1,0:T(8,128)(2,1)} copy(bf16[2,8,2,3,2,128,512]{6,5,4,3,2,0,1:T(8,128)(2,1)} %bitcast.4) | data formatting | bytes 50331648 | tf_op jit(solution)/shard_map/all_to_all | solution.py:92
  589.3 13.4 %gather_fusion.1 = bf16[32,2,128,512]{3,2,1,0:T(8,128)(2,1)} fusion(bf16[2,16,3,2,128,512]{5,4,3,2,1,0:T(8,128)(2,1)} %bitcast.104, s32[32]{0:T(128)S(1)} %reshape.255), kind=kCustom, calls=%fused_computation.3 | custom fusion | bytes 16777600 | tf_op jit(solution)/shard_map/gather | solution.py:93
  602.7 5.9 fusion.43
  608.6 6.2 copy.71
  614.8 3.5 fusion.46
  618.2 0.1 copy.59
  618.3 0.4 fusion.26
  618.8 0.1 copy.65
  618.9 0.1 copy.67
  619.0 0.2 div.22
  619.2 0.1 div.23
  619.3 0.2 mul.88
  619.5 0.1 mul.89
  619.7 0.2 mul.91
  619.9 0.1 mul.92
  620.0 6.2 copy.70
  626.2 8.4 %convolution_bitcast_fusion = f32[2,16,1,4,8,128]{5,4,3,1,0,2:T(8,128)S(1)} fusion(bf16[2,16,128,4,128]{2,4,3,1,0:T(8,128)(2,1)} %bitcast.107, f32[2,16,1,4,8,128]{5,4,3,1,0,2:T(8,128)S(1)} %get-tuple-element.19, f32[2,16,4,8]{3,2,1,0:T(4,128)S(1)} %get-tuple-element.18), kind=kOutput, calls=%fused_computation.16 | convolution fusion | flops 201457664 | bytes 5246976 | tf_op jit(solution)/shard_map/bprkgt,bptkh->bprkgh/dot_general | solution.py:34
  634.7 0.1 reshape_reshape.7
  634.8 0.8 divide_convert_fusion
  (25 shorter events, 0.3 us)
Async XLA Ops:
  0.6 25.1 %copy-start = (s32[16,16]{1,0:T(8,128)S(1)}, s32[16,16]{1,0:T(8,128)}, u32[]{:S(2)}) copy-start(s32[16,16]{1,0:T(8,128)} %param.19) | copy-start | bytes 3076
  17.0 7.9 %copy-start.3 = (s32[16,16,1]{1,2,0:T(1,128)S(1)}, s32[16,16,1]{1,2,0:T(1,128)}, u32[]{:S(2)}) copy-start(s32[16,16,1]{1,2,0:T(1,128)} %param.18) | copy-start | bytes 3076
  17.0 9.6 %copy-start.2 = (bf16[2,16,4096]{2,1,0:T(8,128)(2,1)S(1)}, bf16[2,16,4096]{2,1,0:T(8,128)(2,1)}, u32[]{:S(2)}) copy-start(bf16[2,16,4096]{2,1,0:T(8,128)(2,1)} %param.15) | copy-start | bytes 786436
  17.0 551.6 %all-to-all-start = ((bf16[16,2,3,2,128,512]{5,4,3,2,1,0:T(8,128)(2,1)}), bf16[16,2,3,2,128,512]{5,4,3,2,1,0:T(8,128)(2,1)}, u32[]{:S(2)}, u32[]{:S(2)}) async-start(bf16[16,2,3,2,128,512]{5,4,3,2,1,0:T(8,128)(2,1)} %bitcast.103), calls=%async_computation | async-start | bytes 50331648 | tf_op jit(solution)/shard_map/all_to_all | solution.py:92
  30.5 4.0 copy-start.6
  38.1 5.6 copy-start.4
  38.1 5.6 copy-start.5
  626.2 9.4 %copy-start.1 = (s32[16,16]{1,0:T(8,128)S(1)}, s32[16,16]{1,0:T(8,128)}, u32[]{:S(2)}) copy-start(s32[16,16]{1,0:T(8,128)} %param.19) | copy-start | bytes 3076
where the time goes:
time: 637 us; the launch traced here: 636 us
  waiting for transfers between devices  514 us (81%)
  local copies, waits for them, and re-layouts  80.3 us (13%)
  matrix products  18.2 us (3%)
  other arithmetic  11.2 us (2%)
  starting transfers between devices  7.37 us (1%)
    all_to_all x1, waiting for transfers between devices, body(): lax.all_to_all(outgoing, 'dp', split_axis=0, concat_axis=1, tiled=True)  514 us
    all_to_all x1, local copies, waits for them, and re-layouts, body(): lax.all_to_all(outgoing, 'dp', split_axis=0, concat_axis=1, tiled=True)  20.7 us
    gather x1, local copies, waits for them, and re-layouts, body(): outgoing = caches[resident_ids[None, :, None], sender_pick]  13.9 us
    gather x1, local copies, waits for them, and re-layouts, body(): inherited = arrived[resident_ids[:, None], own_parent, own_slot]  13.4 us
  transfers between devices with their start and end apart: 1, of which 1 were waited for; matrix products, arithmetic and copies ran while one was open for 4% of the time, Pallas kernels for 0%

commit v1 on v0

v1 whole, which is shorter than its diff:
```python
import functools
import math

import jax
import jax.numpy as jnp
from jax import lax
from jax.experimental import pallas as pl
from jax.experimental.pallas import tpu as pltpu
from jax.sharding import PartitionSpec as P

HEAD = 128
D_PRM = 4096
PROB = 16
CTX = 128
STEP = 64
CAP = 3
LANES = 128
MESH = pl.DeviceIdType.MESH


def attend_group(queries, keys, values, limits, block_mask):
    heads = queries[0].shape[0]
    kv_heads = keys[0].shape[1] // HEAD
    group = heads // kv_heads
    count = len(queries)
    scores = []
    for query, key, limit in zip(queries, keys, limits):
        spread = jnp.concatenate([query] * kv_heads, axis=1) * block_mask
        score = lax.dot_general(
            spread, key, (((1,), (1,)), ((), ())), preferred_element_type=jnp.float32
        ) * (1.0 / math.sqrt(HEAD))
        column = lax.broadcasted_iota(jnp.int32, score.shape, 1)
        scores.append(jnp.where(column < limit, score, -1e30))
    scores = jnp.concatenate(scores, axis=0)
    maxima = jnp.max(scores, axis=-1, keepdims=True)
    weights = jnp.exp(scores - maxima)
    totals = jnp.sum(weights, axis=-1, keepdims=True)
    high = weights.astype(jnp.bfloat16)
    low = (weights - high.astype(jnp.float32)).astype(jnp.bfloat16)
    results = []
    for i in range(count):
        rows = slice(i * heads, (i + 1) * heads)
        both = jnp.concatenate([high[rows], low[rows]], axis=0)
        product = lax.dot_general(
            both, values[i], (((1,), (0,)), ((), ())), preferred_element_type=jnp.float32
        )
        product = product[:heads] + product[heads:]
        numerator = jnp.concatenate(
            [
                product[k * group : (k + 1) * group, k * HEAD : (k + 1) * HEAD]
                for k in range(kv_heads)
            ],
            axis=0,
        )
        results.append((numerator, maxima[rows], totals[rows]))
    return results


def kernel(
    n,
    resident,
    table,
    bounds_smem,
    bounds_row,
    queries,
    gain,
    weight,
    hidden,
    step_kv,
    caches,
    out,
    prm,
    hidden_v,
    step_v,
    cache_v,
    sent_q,
    got_q,
    sent_r,
    got_r,
    sent_s,
    got_s,
    own_num,
    own_max,
    own_tot,
    part,
    other,
    load_sem,
    qs_sem,
    qr_sem,
    rs_sem,
    rr_sem,
    ss_sem,
    sr_sem,
    pair_sem,
):
    me = lax.axis_index("dp")
    core = lax.axis_index("tensor")
    rows = resident * PROB
    slots = resident * resident * CAP
    heads = queries.shape[1]
    width = step_v.shape[2]
    kv_heads = width // HEAD
    group = heads // kv_heads
    work_at, len_at, merge_at = n * slots, 2 * n * slots, 3 * n * slots

    chunks = load_sem.shape[1]
    span = rows // chunks

    def load(which, chunk):
        source, target = ((step_kv, step_v), (caches, cache_v), (hidden, hidden_v))[which]
        piece = pl.ds(chunk * span, span)
        return pltpu.make_async_copy(
            source.at[piece], target.at[piece], load_sem.at[which, chunk]
        )

    for which in range(3):
        for chunk in range(chunks):
            load(which, chunk).start()

    barrier = pltpu.get_barrier_semaphore()
    for step in range(1, n):
        pl.semaphore_signal(
            barrier, inc=1, device_id={"dp": lax.rem(me + step, n)}, device_id_type=MESH
        )
    pl.semaphore_signal(barrier, inc=1, device_id={"tensor": 1 - core}, device_id_type=MESH)

    def query_copy(peer, source):
        return pltpu.make_async_remote_copy(
            src_ref=sent_q.at[peer],
            dst_ref=got_q.at[source],
            send_sem=qs_sem.at[peer],
            recv_sem=qr_sem.at[source],
            device_id={"dp": peer},
            device_id_type=MESH,
        )

    def reply_copy(peer, source):
        return pltpu.make_async_remote_copy(
            src_ref=sent_r.at[peer],
            dst_ref=got_r.at[source],
            send_sem=rs_sem.at[peer],
            recv_sem=rr_sem.at[source],
            device_id={"dp": peer},
            device_id_type=MESH,
        )

    def stat_copy(peer, source):
        return pltpu.make_async_remote_copy(
            src_ref=sent_s.at[peer],
            dst_ref=got_s.at[source],
            send_sem=ss_sem.at[peer],
            recv_sem=sr_sem.at[source],
            device_id={"dp": peer},
            device_id_type=MESH,
        )

    def pack(peer, target):
        for slot in range(slots):
            beam = slot // (resident * CAP)
            problem = table[peer * slots + slot]
            target[peer, slot] = queries[beam * PROB + problem]

    pl.semaphore_wait(barrier, n)

    @pl.loop(1, n)
    def _(step):
        peer = lax.rem(me + step, n)
        pack(peer, sent_q)
        query_copy(peer, me).start()

    pack(me, got_q)

    spread_row = lax.broadcasted_iota(jnp.int32, (heads, width), 0)
    spread_col = lax.broadcasted_iota(jnp.int32, (heads, width), 1)
    block_mask = jnp.zeros((heads, width), jnp.float32)
    for k in range(kv_heads):
        inside = (
            (spread_row >= k * group)
            & (spread_row < (k + 1) * group)
            & (spread_col >= k * HEAD)
            & (spread_col < (k + 1) * HEAD)
        )
        block_mask = jnp.where(inside, 1.0, block_mask)
    block_mask = block_mask.astype(jnp.bfloat16)
    stat_row = lax.broadcasted_iota(jnp.int32, (heads, LANES), 0)
    stat_col = lax.broadcasted_iota(jnp.int32, (heads, LANES), 1)

    for chunk in range(chunks):
        load(0, chunk).wait()
    own_batch = 8

    @pl.loop(0, rows // own_batch)
    def _(batch):
        places = [batch * own_batch + i for i in range(own_batch)]
        results = attend_group(
            [queries[j] for j in places],
            [step_v[j, :STEP, :] for j in places],
            [step_v[j, STEP:, :] for j in places],
            [bounds_smem[j] + 1 for j in places],
            block_mask,
        )
        for j, (numerator, maxima, totals) in zip(places, results):
            own_num[j] = numerator
            own_max[j] = jnp.broadcast_to(maxima, (heads, LANES))
            own_tot[j] = jnp.broadcast_to(totals, (heads, LANES))

    for chunk in range(chunks):
        load(1, chunk).wait()

    def serve(peer, reply, stats):
        batch = 6 if slots % 6 == 0 else slots
        for first in range(0, slots, batch):
            numbers = range(first, first + batch)
            places = [
                ((slot // CAP) % resident) * PROB + table[work_at + peer * slots + slot]
                for slot in numbers
            ]
            results = attend_group(
                [got_q[peer, slot] for slot in numbers],
                [cache_v[j, :CTX, :] for j in places],
                [cache_v[j, CTX:, :] for j in places],
                [table[len_at + peer * slots + slot] for slot in numbers],
                block_mask,
            )
            for slot, (numerator, maxima, totals) in zip(numbers, results):
                reply[peer, slot] = numerator
                packed = jnp.where(stat_col == stat_row, maxima, 0.0) + jnp.where(
                    stat_col == stat_row + heads, totals, 0.0
                )
                stats[peer, slot : slot + 1, :] = jnp.sum(packed, axis=0, keepdims=True)

    serve(me, got_r, got_s)

    @pl.loop(1, n)
    def _(step):
        peer = lax.rem(me + n - step, n)
        query_copy(peer, peer).wait_recv()
        serve(peer, sent_r, sent_s)
        reply_copy(peer, me).start()
        stat_copy(peer, me).start()

    for chunk in range(chunks):
        load(2, chunk).wait()
    scaled = gain[...] * weight[...]
    column = lax.broadcasted_iota(jnp.int32, (STEP, LANES), 1)

    def reward(j, carry):
        squares_all, products_all = carry
        wide = hidden_v[j].astype(jnp.float32)
        squares = jnp.sum(wide * wide, axis=-1, keepdims=True)
        products = jnp.sum(wide * scaled, axis=-1, keepdims=True)
        return (
            jnp.where(column == j, squares, squares_all),
            jnp.where(column == j, products, products_all),
        )

    zeros = jnp.zeros((STEP, LANES), jnp.float32)
    squares, products = lax.fori_loop(0, rows, reward, (zeros, zeros))
    part[0] = squares
    part[1] = products
    pair = pltpu.make_async_remote_copy(
        src_ref=part,
        dst_ref=other,
        send_sem=pair_sem.at[0],
        recv_sem=pair_sem.at[1],
        device_id={"tensor": 1 - core},
        device_id_type=MESH,
    )
    pair.start()
    pair.wait()
    squares = part[0] + other[0]
    products = part[1] + other[1]
    token_score = products / jnp.sqrt(squares / D_PRM + 1e-05)
    step_rows = lax.broadcasted_iota(jnp.int32, (STEP, LANES), 0)
    token_score = jnp.where(step_rows <= bounds_row[...], token_score, -1e30)
    prm[...] = jnp.max(token_score, axis=0, keepdims=True)

    @pl.loop(1, n)
    def _(step):
        peer = lax.rem(me + n - step, n)
        reply_copy(peer, peer).wait_recv()
        stat_copy(peer, peer).wait_recv()

    merge_batch = 4

    @pl.loop(0, rows // merge_batch)
    def _(batch):
        for i in range(merge_batch):
            j = batch * merge_batch + i
            source = table[merge_at + 2 * j]
            slot = table[merge_at + 2 * j + 1]
            stats = got_s[source, pl.ds(slot, 1), :]
            cache_max = jnp.sum(
                jnp.where(stat_col == stat_row, stats, 0.0), axis=-1, keepdims=True
            )
            cache_tot = jnp.sum(
                jnp.where(stat_col == stat_row + heads, stats, 0.0), axis=-1, keepdims=True
            )
            highest = jnp.maximum(cache_max, own_max[j])
            scale_cache = jnp.exp(cache_max - highest)
            scale_own = jnp.exp(own_max[j] - highest)
            totals = cache_tot * scale_cache + own_tot[j] * scale_own
            merged = (got_r[source, slot] * scale_cache + own_num[j] * scale_own) / totals
            out[j] = merged.astype(jnp.bfloat16)

    @pl.loop(1, n)
    def _(step):
        peer = lax.rem(me + step, n)
        query_copy(peer, me).wait_send()
        reply_copy(peer, me).wait_send()
        stat_copy(peer, me).wait_send()


def body(
    n,
    step_hidden,
    prm_gain,
    score_weight,
    step_bounds,
    queries,
    step_kv,
    caches,
    parents,
    lengths,
):
    resident = step_hidden.shape[0]
    rows = resident * PROB
    slots = resident * resident * CAP
    heads = queries.shape[-1] // HEAD
    width = caches.shape[-1]
    beams = parents.shape[0]
    me = lax.axis_index("dp")

    parent = parents[:, :, 0]
    problem = jnp.arange(PROB, dtype=jnp.int32)
    siblings = parent[:, :, None] == parent[:, None, :]
    earlier = problem[None, :] < problem[:, None]
    rank = jnp.sum(siblings & earlier[None, :, :], axis=-1, dtype=jnp.int32)
    beam_ids = jnp.arange(beams, dtype=jnp.int32)
    slot_ids = jnp.arange(CAP, dtype=jnp.int32)
    match = (parent[:, None, None, :] == beam_ids[None, :, None, None]) & (
        rank[:, None, None, :] == slot_ids[None, None, :, None]
    )
    pick = jnp.sum(jnp.where(match, problem, 0), axis=-1)
    pick_len = jnp.sum(jnp.where(match, lengths[None, :, None, :], 0), axis=-1)
    first = me * resident
    send = lax.dynamic_slice_in_dim(pick, first, resident, 0)
    send = send.reshape(resident, n, resident, CAP).transpose(1, 0, 2, 3)
    work = lax.dynamic_slice_in_dim(pick, first, resident, 1)
    work_len = lax.dynamic_slice_in_dim(pick_len, first, resident, 1)
    own_parent = lax.dynamic_slice_in_dim(parent, first, resident, 0)
    own_rank = lax.dynamic_slice_in_dim(rank, first, resident, 0)
    local = jnp.arange(resident, dtype=jnp.int32)[:, None]
    source = own_parent // resident
    slot = (local * resident + own_parent % resident) * CAP + own_rank
    merge = jnp.stack([source, slot], axis=-1)
    table = jnp.concatenate(
        [send.reshape(-1), work.reshape(-1), work_len.reshape(-1), merge.reshape(-1)]
    )
    bounds = step_bounds.reshape(-1)
    bounds_row = jnp.pad(bounds, (0, LANES - rows)).reshape(1, LANES)

    smem = pl.BlockSpec(memory_space=pltpu.SMEM)
    vmem = pl.BlockSpec(memory_space=pltpu.VMEM)
    hbm = pl.BlockSpec(memory_space=pl.ANY)
    chunks = 4
    dma = pltpu.SemaphoreType.DMA
    attended, prm = pl.pallas_call(
        functools.partial(kernel, n, resident),
        out_shape=(
            jax.ShapeDtypeStruct((rows, heads, HEAD), jnp.bfloat16),
            jax.ShapeDtypeStruct((1, LANES), jnp.float32),
        ),
        in_specs=[smem, smem, vmem, vmem, vmem, vmem, hbm, hbm, hbm],
        out_specs=(vmem, vmem),
        scratch_shapes=[
            pltpu.VMEM((rows, STEP, step_hidden.shape[-1]), jnp.bfloat16),
            pltpu.VMEM((rows, 2 * STEP, width), jnp.bfloat16),
            pltpu.VMEM((rows, 2 * CTX, width), jnp.bfloat16),
            pltpu.VMEM((n, slots, heads, HEAD), jnp.bfloat16),
            pltpu.VMEM((n, slots, heads, HEAD), jnp.bfloat16),
            pltpu.VMEM((n, slots, heads, HEAD), jnp.float32),
            pltpu.VMEM((n, slots, heads, HEAD), jnp.float32),
            pltpu.VMEM((n, -(-slots // 8) * 8, LANES), jnp.float32),
            pltpu.VMEM((n, -(-slots // 8) * 8, LANES), jnp.float32),
            pltpu.VMEM((rows, heads, HEAD), jnp.float32),
            pltpu.VMEM((rows, heads, LANES), jnp.float32),
            pltpu.VMEM((rows, heads, LANES), jnp.float32),
            pltpu.VMEM((2, STEP, LANES), jnp.float32),
            pltpu.VMEM((2, STEP, LANES), jnp.float32),
            dma((3, chunks)),
            dma((n,)),
            dma((n,)),
            dma((n,)),
            dma((n,)),
            dma((n,)),
            dma((n,)),
            dma((2,)),
        ],
        compiler_params=pltpu.CompilerParams(
            collective_id=0, has_side_effects=True, vmem_limit_bytes=48 * 1024 * 1024
        ),
    )(
        table,
        bounds,
        bounds_row,
        queries.reshape(rows, heads, HEAD),
        prm_gain.reshape(1, -1),
        score_weight.reshape(1, -1),
        step_hidden.reshape(rows, STEP, step_hidden.shape[-1]),
        step_kv.reshape(rows, 2 * STEP, width),
        caches.reshape(rows, 2 * CTX, width),
    )
    attended = attended.reshape(resident, PROB, heads * HEAD)
    return attended, prm[0, :rows].reshape(resident, PROB)


def solution(mesh):
    in_specs = (
        P("dp", "groups", None, "tensor"),
        P("tensor"),
        P("tensor"),
        P("dp", "groups"),
        P("dp", "groups", "tensor"),
        P("dp", "groups", None, None, "tensor"),
        P("dp", "groups", None, None, "tensor"),
        P(None, "groups", None),
        P(None, "groups"),
    )
    out_specs = (P("dp", "groups", "tensor"), P("dp", "groups"))
    return jax.shard_map(
        functools.partial(body, mesh.shape["dp"]),
        mesh=mesh,
        in_specs=in_specs,
        out_specs=out_specs,
        check_vma=False,
    )
```

time: 637 us -> 85.8 us (0.13)
  waiting for transfers between devices: 514 us -> 0 us
  local copies, waits for them, and re-layouts: 80.3 us -> 8.17 us
  Pallas kernels: 0 us -> 70.4 us
  matrix products: 18.2 us -> 0 us
  starting transfers between devices: 7.37 us -> 0 us
    all_to_all x1 -> x0, waiting for transfers between devices: 514 us -> none  [body(): lax.all_to_all(outgoing, 'dp', split_axis=0, concat_axis=1, tiled=True)]
    pallas_call x0 -> x1, Pallas kernels: none -> 70.4 us  [body(): pl.pallas_call(functools.partial(kernel, n, resident), out_shape=(jax.Sha...]
    gather x6 -> x0, local copies, waits for them, and re-layouts: 29.2 us -> none  [the longest x1 13.9 us: body(): outgoing = caches[resident_ids[None, :, None], sender_pick]]
    all_to_all x1 -> x0, local copies, waits for them, and re-layouts: 20.7 us -> none  [body(): lax.all_to_all(outgoing, 'dp', split_axis=0, concat_axis=1, tiled=True)]
    dot_general x4 -> x0, matrix products: 18.2 us -> none  [the longest x2 11.8 us: partial_attend(): jnp.einsum('bprkgt,bptkh->bprkgh', weights, value_heads, precision=lax.Pr...]
    slice x2 -> x1, local copies, waits for them, and re-layouts: 9.82 us -> 0.02 us  [body(): return (attended, prm[0, :rows].reshape(resident, PROB))]
    unnamed x17 -> x7, local copies, waits for them, and re-layouts: 12.5 us -> 4.57 us
    all_to_all x1 -> x0, starting transfers between devices: 7.37 us -> none  [body(): lax.all_to_all(outgoing, 'dp', split_axis=0, concat_axis=1, tiled=True)]
  transfers between devices with their start and end apart: 1 -> 0, of which waited for: 1 -> 0; matrix products, arithmetic and copies ran while one was open for 4% -> 0% of each run, Pallas kernels for 0% -> 0%
where the time goes in v1:
time: 85.8 us; the launch traced here: 85.2 us
  Pallas kernels  70.4 us (82%)
  local copies, waits for them, and re-layouts  8.17 us (10%)
  other arithmetic  5.91 us (7%)
    pallas_call x1, Pallas kernels, body(): pl.pallas_call(functools.partial(kernel, n, resident), out_shape=(jax.Sha...  70.4 us
    unnamed x7, local copies, waits for them, and re-layouts  4.57 us
    reduce_sum x1, other arithmetic, body(): pick = jnp.sum(jnp.where(match, problem, 0), axis=-1)  2.41 us

profile of v1, /device:TPU:0, one launch (start us, length us, event | category | flops | bytes accessed | tf_op | source)
XLA Modules:
  0.0 85.2 jit_solution(3969708605885545787)
XLA Ops:
  0.6 0.8 reshape.87.bounds_smem
  1.4 0.7 and_select_fusion.3
  2.1 1.2 %convert_reduce_fusion = s32[16,16]{1,0:T(8,128)S(1)} fusion(s32[16,16]{1,0:T(8,128)} %bitcast.28, pred[16,16]{1,0:T(8,128)(4,1)S(1)} %iota_compare_fusion.2), kind=kLoop, calls=%fused_computation.4 | loop fusion | flops 16128 | bytes 2304 | tf_op jit(solution)/shard_map/reduce_sum | solution.py:338
  3.3 0.8 fusion.3
  4.1 0.1 copy.24
  4.2 0.1 reshape.86
  4.3 0.7 iota_compare_fusion
  5.0 2.4 %fusion = (s32[16,16,3]{1,2,0:T(4,128)S(1)}, s32[16,16,3]{1,2,0:T(4,128)S(1)}) fusion(pred[16,3,16]{2,1,0:T(4,128)(4,1)S(1)} %iota_compare_fusion.1, pred[16,16,16]{2,1,0:T(8,128)(4,1)S(1)} %iota_compare_fusion, s32[16,16]{1,0:T(8,128)} %param.17), kind=kLoop, calls=%fused_computation.2 | loop fusion | flops 59904 | bytes 12032 | tf_op jit(solution)/shard_map/reduce_sum | solution.py:344
  7.5 0.1 constant_dynamic-slice_fusion.2
  7.6 0.2 copy.22
  7.8 0.1 reshape.85
  7.9 0.2 copy.21
  8.1 0.1 reshape.84
  8.2 0.1 reshape.82
  8.3 0.2 copy.20
  8.5 0.1 reshape.83
  8.6 0.1 pad_add_fusion.1.table
  8.7 1.0 %copy.25 = bf16[4,8,32,128]{3,2,1,0:T(8,128)(2,1)S(1)} copy(bf16[4,8,32,128]{3,1,2,0:T(8,128)(2,1)} %bitcast.25) | data formatting | bytes 524288
  9.7 0.0 copy-start
  9.7 2.2 %copy-done = bf16[2,16,2,64,512]{4,3,2,1,0:T(8,128)(2,1)S(1)} copy-done((bf16[2,16,2,64,512]{4,3,2,1,0:T(8,128)(2,1)S(1)}, bf16[2,16,2,64,512]{4,3,2,1,0:T(8,128)(2,1)}, u32[]{:S(2)}) %copy-start) | copy-done | bytes 4194328
  11.9 0.0 copy-start.1
  11.9 0.7 copy-done.1
  12.6 0.0 copy-start.2
  12.6 0.7 copy-done.2
  13.3 70.4 %shard_map.104 = (bf16[32,32,128]{2,1,0:T(8,128)(2,1)S(1)}, f32[1,128]{1,0:T(1,128)S(1)}) custom-call(s32[352]{0:T(512)S(1)} %pad_add_fusion.1.table, s32[32]{0:T(128)S(1)} %reshape.87.bounds_smem, s32[1,128]{1,0:T(1,128)S(1)} %pad_bitcast_fusion.bounds_row, bf16[32,32,128]{2,1,0:T(8,128)(2,1)S(1)} %bitcast.20, f32[1,2048]{1,0:T(1,128)S(1)} %bitcast.21, ...), custom_call_target="tpu_custom_call" | custom-call | tf_op jit(solution)/shard_map/pallas_call | solution.py:368
  83.7 0.8 reshape.95
  84.5 0.6 reshape_squeeze.3
  (8 shorter events, 0.1 us)
Async XLA Ops:
  9.7 2.2 %copy-start = (bf16[2,16,2,64,512]{4,3,2,1,0:T(8,128)(2,1)S(1)}, bf16[2,16,2,64,512]{4,3,2,1,0:T(8,128)(2,1)}, u32[]{:S(2)}) copy-start(bf16[2,16,2,64,512]{4,3,2,1,0:T(8,128)(2,1)} %param.14) | copy-start | bytes 12582916
  11.9 0.7 copy-start.1
  12.6 0.7 copy-start.2

commit v2 on v1

--- a/solution.py
+++ b/solution.py
@@ -15,6 +15,7 @@
 STEP = 64
 CAP = 3
 LANES = 128
+CODES = 32767.0
 MESH = pl.DeviceIdType.MESH
 
 
@@ -223,10 +224,13 @@
                 block_mask,
             )
             for slot, (numerator, maxima, totals) in zip(numbers, results):
-                reply[peer, slot] = numerator
-                packed = jnp.where(stat_col == stat_row, maxima, 0.0) + jnp.where(
-                    stat_col == stat_row + heads, totals, 0.0
-                )
+                largest = jnp.max(jnp.abs(numerator), axis=-1, keepdims=True)
+                largest = jnp.maximum(largest, 1e-20)
+                coded = jnp.round(numerator * (CODES / largest))
+                reply[peer, slot] = coded.astype(jnp.int32).astype(jnp.int16)
+                packed = jnp.where(stat_col == stat_row, maxima, 0.0)
+                packed = jnp.where(stat_col == stat_row + heads, totals, packed)
+                packed = jnp.where(stat_col == stat_row + 2 * heads, largest, packed)
                 stats[peer, slot : slot + 1, :] = jnp.sum(packed, axis=0, keepdims=True)
 
     serve(me, got_r, got_s)
@@ -296,11 +300,16 @@
             cache_tot = jnp.sum(
                 jnp.where(stat_col == stat_row + heads, stats, 0.0), axis=-1, keepdims=True
             )
+            cache_step = jnp.sum(
+                jnp.where(stat_col == stat_row + 2 * heads, stats, 0.0), axis=-1, keepdims=True
+            ) * (1.0 / CODES)
             highest = jnp.maximum(cache_max, own_max[j])
             scale_cache = jnp.exp(cache_max - highest)
             scale_own = jnp.exp(own_max[j] - highest)
             totals = cache_tot * scale_cache + own_tot[j] * scale_own
-            merged = (got_r[source, slot] * scale_cache + own_num[j] * scale_own) / totals
+            coded = got_r[source, slot].astype(jnp.int32).astype(jnp.float32)
+            cache_num = coded * (cache_step * scale_cache)
+            merged = (cache_num + own_num[j] * scale_own) / totals
             out[j] = merged.astype(jnp.bfloat16)
 
     @pl.loop(1, n)
@@ -379,8 +388,8 @@
             pltpu.VMEM((rows, 2 * CTX, width), jnp.bfloat16),
             pltpu.VMEM((n, slots, heads, HEAD), jnp.bfloat16),
             pltpu.VMEM((n, slots, heads, HEAD), jnp.bfloat16),
-            pltpu.VMEM((n, slots, heads, HEAD), jnp.float32),
-            pltpu.VMEM((n, slots, heads, HEAD), jnp.float32),
+            pltpu.VMEM((n, slots, heads, HEAD), jnp.int16),
+            pltpu.VMEM((n, slots, heads, HEAD), jnp.int16),
             pltpu.VMEM((n, -(-slots // 8) * 8, LANES), jnp.float32),
             pltpu.VMEM((n, -(-slots // 8) * 8, LANES), jnp.float32),
             pltpu.VMEM((rows, heads, HEAD), jnp.float32),

time: 85.8 us -> 65.1 us (0.76)
  Pallas kernels: 70.4 us -> 49.7 us
    pallas_call x1, Pallas kernels: 70.4 us -> 49.7 us  [body(): pl.pallas_call(functools.partial(kernel, n, resident), out_shape=(jax.Sha...]
where the time goes in v2:
time: 65.1 us; the launch traced here: 64.5 us
  Pallas kernels  49.7 us (76%)
  local copies, waits for them, and re-layouts  8.17 us (13%)
  other arithmetic  5.91 us (9%)
  between operations  0.73 us (1%)
    pallas_call x1, Pallas kernels, body(): pl.pallas_call(functools.partial(kernel, n, resident), out_shape=(jax.Sha...  49.7 us
    unnamed x7, local copies, waits for them, and re-layouts  4.57 us
    reduce_sum x1, other arithmetic, body(): pick = jnp.sum(jnp.where(match, problem, 0), axis=-1)  2.41 us

profile of v2, /device:TPU:0, one launch (start us, length us, event | category | flops | bytes accessed | tf_op | source)
XLA Modules:
  0.0 64.5 jit_solution(15509484629222092795)
XLA Ops:
  0.6 0.8 %reshape.87.bounds_smem = s32[32]{0:T(128)S(1)} reshape(s32[2,16]{1,0:T(2,128)} %param.12) | data formatting | bytes 256 | tf_op jit(solution)/shard_map/reshape | solution.py:369
  1.4 0.7 %and_select_fusion.3 = s32[2,16,1]{1,0,2:T(2,128)S(1)} fusion(s32[16,16,1]{1,0,2:T(8,128)} %bitcast.27, s32[]{:T(128)S(6)} %select_n.29), kind=kLoop, calls=%fused_computation.13 | loop fusion | flops 480 | bytes 260 | tf_op jit(solution)/shard_map/jit(floor_divide)/jit(_where)/select_n | solution.py:363
  2.1 1.2 %convert_reduce_fusion = s32[16,16]{1,0:T(8,128)S(1)} fusion(s32[16,16]{1,0:T(8,128)} %bitcast.28, pred[16,16]{1,0:T(8,128)(4,1)S(1)} %iota_compare_fusion.2), kind=kLoop, calls=%fused_computation.4 | loop fusion | flops 16128 | bytes 2304 | tf_op jit(solution)/shard_map/reduce_sum | solution.py:347
  3.3 0.8 %fusion.3 = s32[2,16,1]{1,0,2:T(2,128)S(1)} fusion(s32[16,16]{1,0:T(8,128)S(1)} %convert_reduce_fusion, s32[]{:T(128)S(6)} %select_n.29, s32[16,16,1]{1,0,2:T(8,128)} %bitcast.29, s32[2]{0:T(128)S(1)} %iota_multiply_fusion), kind=kLoop, calls=%fused_computation.23 | loop fusion | flops 448 | bytes 396 | tf_op jit(solution)/shard_map/stack | solution.py:365
  4.1 0.1 copy.24
  4.2 0.1 reshape.86
  4.3 0.7 %iota_compare_fusion = pred[16,16,16]{2,1,0:T(8,128)(4,1)S(1)} fusion(s32[16,16]{1,0:T(8,128)} %bitcast.30), kind=kLoop, calls=%fused_computation.5 | loop fusion | flops 4096 | bytes 5120 | tf_op jit(solution)/shard_map/eq | solution.py:350
  5.0 2.4 %fusion = (s32[16,16,3]{1,2,0:T(4,128)S(1)}, s32[16,16,3]{1,2,0:T(4,128)S(1)}) fusion(pred[16,3,16]{2,1,0:T(4,128)(4,1)S(1)} %iota_compare_fusion.1, pred[16,16,16]{2,1,0:T(8,128)(4,1)S(1)} %iota_compare_fusion, s32[16,16]{1,0:T(8,128)} %param.17), kind=kLoop, calls=%fused_computation.2 | loop fusion | flops 59904 | bytes 12032 | tf_op jit(solution)/shard_map/reduce_sum | solution.py:353
  7.5 0.1 constant_dynamic-slice_fusion.2
  7.6 0.2 copy.22
  7.8 0.1 reshape.85
  7.9 0.2 copy.21
  8.1 0.1 reshape.84
  8.2 0.1 reshape.82
  8.3 0.2 copy.20
  8.5 0.1 reshape.83
  8.6 0.1 pad_add_fusion.1.table
  8.7 1.0 %copy.25 = bf16[4,8,32,128]{3,2,1,0:T(8,128)(2,1)S(1)} copy(bf16[4,8,32,128]{3,1,2,0:T(8,128)(2,1)} %bitcast.25) | data formatting | bytes 524288
  9.7 0.0 copy-start
  9.7 2.2 %copy-done = bf16[2,16,2,64,512]{4,3,2,1,0:T(8,128)(2,1)S(1)} copy-done((bf16[2,16,2,64,512]{4,3,2,1,0:T(8,128)(2,1)S(1)}, bf16[2,16,2,64,512]{4,3,2,1,0:T(8,128)(2,1)}, u32[]{:S(2)}) %copy-start) | copy-done | bytes 4194328
  11.9 0.0 copy-start.1
  11.9 0.7 %copy-done.1 = f32[2048]{0:T(1024)S(1)} copy-done((f32[2048]{0:T(1024)S(1)}, f32[2048]{0:T(1024)}, u32[]{:S(2)}) %copy-start.1) | copy-done | bytes 8216
  12.6 0.0 copy-start.2
  12.6 0.7 %copy-done.2 = f32[2048]{0:T(1024)S(1)} copy-done((f32[2048]{0:T(1024)S(1)}, f32[2048]{0:T(1024)}, u32[]{:S(2)}) %copy-start.2) | copy-done | bytes 8216
  13.3 49.7 %shard_map.104 = (bf16[32,32,128]{2,1,0:T(8,128)(2,1)S(1)}, f32[1,128]{1,0:T(1,128)S(1)}) custom-call(s32[352]{0:T(512)S(1)} %pad_add_fusion.1.table, s32[32]{0:T(128)S(1)} %reshape.87.bounds_smem, s32[1,128]{1,0:T(1,128)S(1)} %pad_bitcast_fusion.bounds_row, bf16[32,32,128]{2,1,0:T(8,128)(2,1)S(1)} %bitcast.20, f32[1,2048]{1,0:T(1,128)S(1)} %bitcast.21, ...), custom_call_target="tpu_custom_call" | custom-call | tf_op jit(solution)/shard_map/pallas_call | solution.py:377
  63.0 0.8 %reshape.95 = bf16[2,16,4096]{2,1,0:T(8,128)(2,1)} reshape(bf16[32,32,128]{2,1,0:T(8,128)(2,1)S(1)} %get-tuple-element.4) | data formatting | bytes 524288 | tf_op jit(solution)/shard_map/reshape | solution.py:423
  63.9 0.6 reshape_squeeze.3
  (8 shorter events, 0.1 us)
Async XLA Ops:
  9.7 2.2 %copy-start = (bf16[2,16,2,64,512]{4,3,2,1,0:T(8,128)(2,1)S(1)}, bf16[2,16,2,64,512]{4,3,2,1,0:T(8,128)(2,1)}, u32[]{:S(2)}) copy-start(bf16[2,16,2,64,512]{4,3,2,1,0:T(8,128)(2,1)} %param.14) | copy-start | bytes 12582916
  11.9 0.7 %copy-start.1 = (f32[2048]{0:T(1024)S(1)}, f32[2048]{0:T(1024)}, u32[]{:S(2)}) copy-start(f32[2048]{0:T(1024)} %param.10) | copy-start | bytes 24580
  12.6 0.7 %copy-start.2 = (f32[2048]{0:T(1024)S(1)}, f32[2048]{0:T(1024)}, u32[]{:S(2)}) copy-start(f32[2048]{0:T(1024)} %param.11) | copy-start | bytes 24580

commit v3 on v2

--- a/solution.py
+++ b/solution.py
@@ -60,17 +60,24 @@
 def kernel(
     n,
     resident,
-    table,
     bounds_smem,
-    bounds_row,
     queries,
     gain,
     weight,
+    parents,
+    lengths,
     hidden,
     step_kv,
     caches,
     out,
     prm,
+    gain_v,
+    weight_v,
+    parent_v,
+    length_v,
+    rank_v,
+    table_v,
+    table,
     hidden_v,
     step_v,
     cache_v,
@@ -85,6 +92,7 @@
     own_tot,
     part,
     other,
+    small_sem,
     load_sem,
     qs_sem,
     qr_sem,
@@ -102,7 +110,7 @@
     width = step_v.shape[2]
     kv_heads = width // HEAD
     group = heads // kv_heads
-    work_at, len_at, merge_at = n * slots, 2 * n * slots, 3 * n * slots
+    beams = n * resident
 
     chunks = load_sem.shape[1]
     span = rows // chunks
@@ -114,6 +122,14 @@
             source.at[piece], target.at[piece], load_sem.at[which, chunk]
         )
 
+    small = [
+        pltpu.make_async_copy(source, target, small_sem.at[i])
+        for i, (source, target) in enumerate(
+            ((parents, parent_v), (lengths, length_v), (gain, gain_v), (weight, weight_v))
+        )
+    ]
+    for copy in small:
+        copy.start()
     for which in range(3):
         for chunk in range(chunks):
             load(which, chunk).start()
@@ -158,8 +174,46 @@
     def pack(peer, target):
         for slot in range(slots):
             beam = slot // (resident * CAP)
-            problem = table[peer * slots + slot]
+            near = slot // CAP % resident
+            problem = table[peer * resident + near, beam * CAP + slot % CAP]
             target[peer, slot] = queries[beam * PROB + problem]
+
+    small[0].wait()
+    small[1].wait()
+    table_v[...] = jnp.zeros_like(table_v)
+    parent = parent_v[...]
+    problem_ids = lax.broadcasted_iota(jnp.int32, parent.shape, 1)
+    beam_ids = lax.broadcasted_iota(jnp.int32, parent.shape, 0)
+    rank = jnp.zeros_like(parent)
+    for p in range(PROB - 1):
+        sibling = (parent == parent[:, p : p + 1]) & (problem_ids > p)
+        rank = rank + jnp.where(sibling, 1, 0)
+    rank_v[...] = rank
+    places = lax.broadcasted_iota(jnp.int32, (beams, LANES), 1)
+    to_send = jnp.zeros((beams, LANES), jnp.int32)
+    to_serve = jnp.zeros((beams, LANES), jnp.int32)
+    live = jnp.zeros((beams, LANES), jnp.int32)
+    for beam in range(resident):
+        own = pl.ds(me * resident + beam, 1)
+        own_parent, own_rank, own_length = parent_v[own, :], rank_v[own, :], length_v[own, :]
+        for k in range(CAP):
+            here = places == beam * CAP + k
+            match = (own_parent == beam_ids) & (own_rank == k)
+            found = jnp.sum(jnp.where(match, problem_ids, 0), axis=1, keepdims=True)
+            to_send = jnp.where(here, found, to_send)
+            match = (parent == me * resident + beam) & (rank == k)
+            found = jnp.sum(jnp.where(match, problem_ids, 0), axis=1, keepdims=True)
+            to_serve = jnp.where(here, found, to_serve)
+            found = jnp.sum(jnp.where(match, own_length, 0), axis=1, keepdims=True)
+            live = jnp.where(here, found, live)
+    table_v[0:beams, :] = to_send
+    table_v[beams : 2 * beams, :] = to_serve
+    table_v[2 * beams : 3 * beams, :] = live
+    table_v[3 * beams : 4 * beams, 0:PROB] = rank
+    table_v[4 * beams : 5 * beams, 0:PROB] = parent
+    to_scalar = pltpu.make_async_copy(table_v, table, small_sem.at[4])
+    to_scalar.start()
+    to_scalar.wait()
 
     pl.semaphore_wait(barrier, n)
 
@@ -197,7 +251,7 @@
             [queries[j] for j in places],
             [step_v[j, :STEP, :] for j in places],
             [step_v[j, STEP:, :] for j in places],
-            [bounds_smem[j] + 1 for j in places],
+            [bounds_smem[lax.div(j, PROB), lax.rem(j, PROB)] + 1 for j in places],
             block_mask,
         )
         for j, (numerator, maxima, totals) in zip(places, results):
@@ -212,15 +266,22 @@
         batch = 6 if slots % 6 == 0 else slots
         for first in range(0, slots, batch):
             numbers = range(first, first + batch)
+            cells = [
+                (
+                    peer * resident + slot // (resident * CAP),
+                    slot // CAP % resident * CAP + slot % CAP,
+                )
+                for slot in numbers
+            ]
             places = [
-                ((slot // CAP) % resident) * PROB + table[work_at + peer * slots + slot]
-                for slot in numbers
+                slot // CAP % resident * PROB + table[beams + row, cell]
+                for slot, (row, cell) in zip(numbers, cells)
             ]
             results = attend_group(
                 [got_q[peer, slot] for slot in numbers],
                 [cache_v[j, :CTX, :] for j in places],
                 [cache_v[j, CTX:, :] for j in places],
-                [table[len_at + peer * slots + slot] for slot in numbers],
+                [table[2 * beams + row, cell] for row, cell in cells],
                 block_mask,
             )
             for slot, (numerator, maxima, totals) in zip(numbers, results):
@@ -245,7 +306,13 @@
 
     for chunk in range(chunks):
         load(2, chunk).wait()
-    scaled = gain[...] * weight[...]
+    small[2].wait()
+    small[3].wait()
+    scaled = gain_v[...] * weight_v[...]
+    lane = lax.broadcasted_iota(jnp.int32, (1, LANES), 1)
+    last_row = jnp.zeros((1, LANES), jnp.int32)
+    for j in range(rows):
+        last_row = jnp.where(lane == j, bounds_smem[j // PROB, j % PROB], last_row)
     column = lax.broadcasted_iota(jnp.int32, (STEP, LANES), 1)
 
     def reward(j, carry):
@@ -276,8 +343,10 @@
     products = part[1] + other[1]
     token_score = products / jnp.sqrt(squares / D_PRM + 1e-05)
     step_rows = lax.broadcasted_iota(jnp.int32, (STEP, LANES), 0)
-    token_score = jnp.where(step_rows <= bounds_row[...], token_score, -1e30)
-    prm[...] = jnp.max(token_score, axis=0, keepdims=True)
+    token_score = jnp.where(step_rows <= last_row, token_score, -1e30)
+    best = jnp.max(token_score, axis=0, keepdims=True)
+    for beam in range(resident):
+        prm[beam : beam + 1, :] = best[:, beam * PROB : (beam + 1) * PROB]
 
     @pl.loop(1, n)
     def _(step):
@@ -291,8 +360,11 @@
     def _(batch):
         for i in range(merge_batch):
             j = batch * merge_batch + i
-            source = table[merge_at + 2 * j]
-            slot = table[merge_at + 2 * j + 1]
+            beam, problem = lax.div(j, PROB), lax.rem(j, PROB)
+            ancestor = table[4 * beams + me * resident + beam, problem]
+            place = jnp.minimum(table[3 * beams + me * resident + beam, problem], CAP - 1)
+            source = lax.div(ancestor, resident)
+            slot = (beam * resident + lax.rem(ancestor, resident)) * CAP + place
             stats = got_s[source, pl.ds(slot, 1), :]
             cache_max = jnp.sum(
                 jnp.where(stat_col == stat_row, stats, 0.0), axis=-1, keepdims=True
@@ -338,37 +410,6 @@
     heads = queries.shape[-1] // HEAD
     width = caches.shape[-1]
     beams = parents.shape[0]
-    me = lax.axis_index("dp")
-
-    parent = parents[:, :, 0]
-    problem = jnp.arange(PROB, dtype=jnp.int32)
-    siblings = parent[:, :, None] == parent[:, None, :]
-    earlier = problem[None, :] < problem[:, None]
-    rank = jnp.sum(siblings & earlier[None, :, :], axis=-1, dtype=jnp.int32)
-    beam_ids = jnp.arange(beams, dtype=jnp.int32)
-    slot_ids = jnp.arange(CAP, dtype=jnp.int32)
-    match = (parent[:, None, None, :] == beam_ids[None, :, None, None]) & (
-        rank[:, None, None, :] == slot_ids[None, None, :, None]
-    )
-    pick = jnp.sum(jnp.where(match, problem, 0), axis=-1)
-    pick_len = jnp.sum(jnp.where(match, lengths[None, :, None, :], 0), axis=-1)
-    first = me * resident
-    send = lax.dynamic_slice_in_dim(pick, first, resident, 0)
-    send = send.reshape(resident, n, resident, CAP).transpose(1, 0, 2, 3)
-    work = lax.dynamic_slice_in_dim(pick, first, resident, 1)
-    work_len = lax.dynamic_slice_in_dim(pick_len, first, resident, 1)
-    own_parent = lax.dynamic_slice_in_dim(parent, first, resident, 0)
-    own_rank = lax.dynamic_slice_in_dim(rank, first, resident, 0)
-    local = jnp.arange(resident, dtype=jnp.int32)[:, None]
-    source = own_parent // resident
-    slot = (local * resident + own_parent % resident) * CAP + own_rank
-    merge = jnp.stack([source, slot], axis=-1)
-    table = jnp.concatenate(
-        [send.reshape(-1), work.reshape(-1), work_len.reshape(-1), merge.reshape(-1)]
-    )
-    bounds = step_bounds.reshape(-1)
-    bounds_row = jnp.pad(bounds, (0, LANES - rows)).reshape(1, LANES)
-
     smem = pl.BlockSpec(memory_space=pltpu.SMEM)
     vmem = pl.BlockSpec(memory_space=pltpu.VMEM)
     hbm = pl.BlockSpec(memory_space=pl.ANY)
@@ -378,11 +419,18 @@
         functools.partial(kernel, n, resident),
         out_shape=(
             jax.ShapeDtypeStruct((rows, heads, HEAD), jnp.bfloat16),
-            jax.ShapeDtypeStruct((1, LANES), jnp.float32),
+            jax.ShapeDtypeStruct((resident, PROB), jnp.float32),
         ),
-        in_specs=[smem, smem, vmem, vmem, vmem, vmem, hbm, hbm, hbm],
+        in_specs=[smem, vmem] + [hbm] * 7,
         out_specs=(vmem, vmem),
         scratch_shapes=[
+            pltpu.VMEM((1, prm_gain.shape[0]), jnp.float32),
+            pltpu.VMEM((1, prm_gain.shape[0]), jnp.float32),
+            pltpu.VMEM((beams, PROB), jnp.int32),
+            pltpu.VMEM((beams, PROB), jnp.int32),
+            pltpu.VMEM((beams, PROB), jnp.int32),
+            pltpu.VMEM((5 * beams, LANES), jnp.int32),
+            pltpu.SMEM((5 * beams, LANES), jnp.int32),
             pltpu.VMEM((rows, STEP, step_hidden.shape[-1]), jnp.bfloat16),
             pltpu.VMEM((rows, 2 * STEP, width), jnp.bfloat16),
             pltpu.VMEM((rows, 2 * CTX, width), jnp.bfloat16),
@@ -397,6 +445,7 @@
             pltpu.VMEM((rows, heads, LANES), jnp.float32),
             pltpu.VMEM((2, STEP, LANES), jnp.float32),
             pltpu.VMEM((2, STEP, LANES), jnp.float32),
+            dma((5,)),
             dma((3, chunks)),
             dma((n,)),
             dma((n,)),
@@ -407,21 +456,21 @@
             dma((2,)),
         ],
         compiler_params=pltpu.CompilerParams(
-            collective_id=0, has_side_effects=True, vmem_limit_bytes=48 * 1024 * 1024
+            collective_id=0, has_side_effects=True, vmem_limit_bytes=60 * 1024 * 1024
         ),
     )(
-        table,
-        bounds,
-        bounds_row,
+        step_bounds,
         queries.reshape(rows, heads, HEAD),
         prm_gain.reshape(1, -1),
         score_weight.reshape(1, -1),
+        parents[:, :, 0],
+        lengths,
         step_hidden.reshape(rows, STEP, step_hidden.shape[-1]),
         step_kv.reshape(rows, 2 * STEP, width),
         caches.reshape(rows, 2 * CTX, width),
     )
     attended = attended.reshape(resident, PROB, heads * HEAD)
-    return attended, prm[0, :rows].reshape(resident, PROB)
+    return attended, prm
 
 
 def solution(mesh):

time: 65.1 us -> 60.1 us (0.923)
  other arithmetic: 5.91 us -> 0 us
  Pallas kernels: 49.7 us -> 54.5 us
  local copies, waits for them, and re-layouts: 8.17 us -> 4.7 us
    pallas_call x1, Pallas kernels: 49.7 us -> 54.5 us  [body(): pl.pallas_call(functools.partial(kernel, n, resident), out_shape=(jax.Sha...]
    reduce_sum x2 -> x0, other arithmetic: 3.61 us -> none  [the longest x1 2.41 us: body(): pick = jnp.sum(jnp.where(match, problem, 0), axis=-1)]
    unnamed x7 -> x2, local copies, waits for them, and re-layouts: 4.57 us -> 2.93 us
    reshape x7 -> x0, local copies, waits for them, and re-layouts: 1.3 us -> none  [the longest x1 0.76 us: body(): bounds = step_bounds.reshape(-1)]
    reshape x1, local copies, waits for them, and re-layouts: 0.82 us -> 1.77 us  [body(): attended = attended.reshape(resident, PROB, heads * HEAD)]
    another operation x2 -> x0, other arithmetic: 0.77 us -> none  [body(): merge = jnp.stack([source, slot], axis=-1)]
    eq x2 -> x0, other arithmetic: 0.74 us -> none  [the longest x1 0.72 us: body(): parent[:, None, None, :] == beam_ids[None, :, None, None]]
    another operation x2 -> x0, local copies, waits for them, and re-layouts: 0.73 us -> none  [the longest x1 0.64 us: body(): return (attended, prm[0, :rows].reshape(resident, PROB))]
where the time goes in v3:
time: 60.1 us; the launch traced here: 59.9 us
  Pallas kernels  54.5 us (91%)
  local copies, waits for them, and re-layouts  4.7 us (8%)
  between operations  0.64 us (1%)
    pallas_call x1, Pallas kernels, body(): pl.pallas_call(functools.partial(kernel, n, resident), out_shape=(jax.Sha...  54.5 us
    unnamed x2, local copies, waits for them, and re-layouts  2.93 us
    reshape x1, local copies, waits for them, and re-layouts, body(): attended = attended.reshape(resident, PROB, heads * HEAD)  1.77 us

profile of v3, /device:TPU:0, one launch (start us, length us, event | category | flops | bytes accessed | tf_op | source)
XLA Modules:
  0.0 59.9 jit_solution(8463075167976308781)
XLA Ops:
  0.6 1.7 %copy.11 = bf16[4,8,32,128]{3,2,1,0:T(8,128)(2,1)} copy(bf16[4,8,32,128]{3,1,2,0:T(8,128)(2,1)} %bitcast.13) | data formatting | bytes 524288
  2.3 54.5 %shard_map.104 = (bf16[32,32,128]{2,1,0:T(8,128)(2,1)}, f32[2,16]{1,0:T(2,128)}) custom-call(s32[2,16]{1,0:T(2,128)} %bounds_smem.1, bf16[32,32,128]{2,1,0:T(8,128)(2,1)} %bitcast.12, f32[1,2048]{1,0:T(1,128)} %bitcast.14, f32[1,2048]{1,0:T(1,128)} %bitcast.15, s32[16,16]{1,0:T(8,128)} %bitcast.16, s32[16,16]{1,0:T(8,128)} %lengths.1, ...), custom_call_target="tpu_custom_call" | custom-call | tf_op jit(solution)/shard_map/pallas_call | solution.py:418
  56.9 1.8 %reshape.31 = bf16[2,16,4096]{2,1,0:T(8,128)(2,1)} reshape(bf16[32,32,128]{2,1,0:T(8,128)(2,1)} %get-tuple-element.4) | data formatting | bytes 524288 | tf_op jit(solution)/shard_map/reshape | solution.py:472
  58.6 1.2 %copy.13 = f32[2,16]{1,0:T(2,128)} copy(f32[2,16]{1,0:T(2,128)} %get-tuple-element.9) | data formatting | bytes 256

commit v4 on v3

--- a/solution.py
+++ b/solution.py
@@ -141,6 +141,9 @@
         )
     pl.semaphore_signal(barrier, inc=1, device_id={"tensor": 1 - core}, device_id_type=MESH)
 
+    def offset(step):
+        return n // 2 + lax.div(step, 2) * (2 * lax.rem(step, 2) - 1)
+
     def query_copy(peer, source):
         return pltpu.make_async_remote_copy(
             src_ref=sent_q.at[peer],
@@ -219,7 +222,7 @@
 
     @pl.loop(1, n)
     def _(step):
-        peer = lax.rem(me + step, n)
+        peer = lax.rem(me + offset(step), n)
         pack(peer, sent_q)
         query_copy(peer, me).start()
 
@@ -298,7 +301,7 @@
 
     @pl.loop(1, n)
     def _(step):
-        peer = lax.rem(me + n - step, n)
+        peer = lax.rem(me + n - offset(step), n)
         query_copy(peer, peer).wait_recv()
         serve(peer, sent_r, sent_s)
         reply_copy(peer, me).start()

time: 60.1 us -> 55 us (0.915)
  Pallas kernels: 54.5 us -> 49.4 us
    pallas_call x1, Pallas kernels: 54.5 us -> 49.4 us  [body(): pl.pallas_call(functools.partial(kernel, n, resident), out_shape=(jax.Sha...]
where the time goes in v4:
time: 55 us; the launch traced here: 54.8 us
  Pallas kernels  49.4 us (90%)
  local copies, waits for them, and re-layouts  4.7 us (9%)
  between operations  0.64 us (1%)
    pallas_call x1, Pallas kernels, body(): pl.pallas_call(functools.partial(kernel, n, resident), out_shape=(jax.Sha...  49.4 us
    unnamed x2, local copies, waits for them, and re-layouts  2.93 us
    reshape x1, local copies, waits for them, and re-layouts, body(): attended = attended.reshape(resident, PROB, heads * HEAD)  1.77 us

profile of v4, /device:TPU:0, one launch (start us, length us, event | category | flops | bytes accessed | tf_op | source)
XLA Modules:
  0.0 54.8 jit_solution(14512810887803478406)
XLA Ops:
  0.6 1.7 %copy.11 = bf16[4,8,32,128]{3,2,1,0:T(8,128)(2,1)} copy(bf16[4,8,32,128]{3,1,2,0:T(8,128)(2,1)} %bitcast.13) | data formatting | bytes 524288
  2.3 49.4 %shard_map.104 = (bf16[32,32,128]{2,1,0:T(8,128)(2,1)}, f32[2,16]{1,0:T(2,128)}) custom-call(s32[2,16]{1,0:T(2,128)} %bounds_smem.1, bf16[32,32,128]{2,1,0:T(8,128)(2,1)} %bitcast.12, f32[1,2048]{1,0:T(1,128)} %bitcast.14, f32[1,2048]{1,0:T(1,128)} %bitcast.15, s32[16,16]{1,0:T(8,128)} %bitcast.16, s32[16,16]{1,0:T(8,128)} %lengths.1, ...), custom_call_target="tpu_custom_call" | custom-call | tf_op jit(solution)/shard_map/pallas_call | solution.py:421
  51.8 1.8 %reshape.31 = bf16[2,16,4096]{2,1,0:T(8,128)(2,1)} reshape(bf16[32,32,128]{2,1,0:T(8,128)(2,1)} %get-tuple-element.4) | data formatting | bytes 524288 | tf_op jit(solution)/shard_map/reshape | solution.py:475
  53.6 1.2 %copy.13 = f32[2,16]{1,0:T(2,128)} copy(f32[2,16]{1,0:T(2,128)} %get-tuple-element.9) | data formatting | bytes 256

commit v5 on v4

--- a/solution.py
+++ b/solution.py
@@ -347,9 +347,7 @@
     token_score = products / jnp.sqrt(squares / D_PRM + 1e-05)
     step_rows = lax.broadcasted_iota(jnp.int32, (STEP, LANES), 0)
     token_score = jnp.where(step_rows <= last_row, token_score, -1e30)
-    best = jnp.max(token_score, axis=0, keepdims=True)
-    for beam in range(resident):
-        prm[beam : beam + 1, :] = best[:, beam * PROB : (beam + 1) * PROB]
+    prm[...] = jnp.max(token_score, axis=0, keepdims=True)
 
     @pl.loop(1, n)
     def _(step):
@@ -422,7 +420,7 @@
         functools.partial(kernel, n, resident),
         out_shape=(
             jax.ShapeDtypeStruct((rows, heads, HEAD), jnp.bfloat16),
-            jax.ShapeDtypeStruct((resident, PROB), jnp.float32),
+            jax.ShapeDtypeStruct((1, LANES), jnp.float32),
         ),
         in_specs=[smem, vmem] + [hbm] * 7,
         out_specs=(vmem, vmem),
@@ -459,7 +457,7 @@
             dma((2,)),
         ],
         compiler_params=pltpu.CompilerParams(
-            collective_id=0, has_side_effects=True, vmem_limit_bytes=60 * 1024 * 1024
+            collective_id=0, has_side_effects=True, vmem_limit_bytes=54400 * 1024
         ),
     )(
         step_bounds,
@@ -473,7 +471,7 @@
         caches.reshape(rows, 2 * CTX, width),
     )
     attended = attended.reshape(resident, PROB, heads * HEAD)
-    return attended, prm
+    return attended, prm[0, :rows].reshape(resident, PROB)
 
 
 def solution(mesh):

time: 55 us -> 51.4 us (0.935)
  Pallas kernels: 49.4 us -> 44.4 us
  local copies, waits for them, and re-layouts: 4.7 us -> 5.93 us
    pallas_call x1, Pallas kernels: 49.4 us -> 44.4 us  [body(): pl.pallas_call(functools.partial(kernel, n, resident), out_shape=(jax.Sha...]
    unnamed x2 -> x11, local copies, waits for them, and re-layouts: 2.93 us -> 4.45 us
    reshape x1, local copies, waits for them, and re-layouts: 1.77 us -> 0.82 us  [body(): attended = attended.reshape(resident, PROB, heads * HEAD)]
    another operation x0 -> x1, local copies, waits for them, and re-layouts: none -> 0.64 us  [body(): return (attended, prm[0, :rows].reshape(resident, PROB))]
where the time goes in v5:
time: 51.4 us; the launch traced here: 51 us
  Pallas kernels  44.4 us (86%)
  local copies, waits for them, and re-layouts  5.93 us (12%)
  between operations  0.66 us (1%)
    pallas_call x1, Pallas kernels, body(): pl.pallas_call(functools.partial(kernel, n, resident), out_shape=(jax.Sha...  44.4 us
    unnamed x11, local copies, waits for them, and re-layouts  4.45 us

profile of v5, /device:TPU:0, one launch (start us, length us, event | category | flops | bytes accessed | tf_op | source)
XLA Modules:
  0.0 51.0 jit_solution(7348845182856276133)
XLA Ops:
  0.6 1.0 %copy.11 = bf16[4,8,32,128]{3,2,1,0:T(8,128)(2,1)S(1)} copy(bf16[4,8,32,128]{3,1,2,0:T(8,128)(2,1)} %bitcast.16) | data formatting | bytes 524288
  1.6 0.0 copy-start
  1.6 0.7 %copy-done = f32[2048]{0:T(1024)S(1)} copy-done((f32[2048]{0:T(1024)S(1)}, f32[2048]{0:T(1024)}, u32[]{:S(2)}) %copy-start) | copy-done | bytes 8216
  2.3 0.0 copy-start.1
  2.3 0.7 %copy-done.1 = f32[2048]{0:T(1024)S(1)} copy-done((f32[2048]{0:T(1024)S(1)}, f32[2048]{0:T(1024)}, u32[]{:S(2)}) %copy-start.1) | copy-done | bytes 8216
  3.0 0.0 copy-start.2
  3.0 0.7 %copy-done.2 = s32[16,16,1]{1,2,0:T(1,128)S(1)} copy-done((s32[16,16,1]{1,2,0:T(1,128)S(1)}, s32[16,16,1]{1,2,0:T(1,128)}, u32[]{:S(2)}) %copy-start.2) | copy-done | bytes 1048
  3.7 0.0 copy-start.3
  3.7 0.7 %copy-done.3 = s32[16,16]{1,0:T(8,128)S(1)} copy-done((s32[16,16]{1,0:T(8,128)S(1)}, s32[16,16]{1,0:T(8,128)}, u32[]{:S(2)}) %copy-start.3) | copy-done | bytes 1048
  4.4 0.0 copy-start.4
  4.4 0.7 %copy-done.4 = s32[2,16]{1,0:T(2,128)S(1)} copy-done((s32[2,16]{1,0:T(2,128)S(1)}, s32[2,16]{1,0:T(2,128)}, u32[]{:S(2)}) %copy-start.4) | copy-done | bytes 152
  5.1 44.4 %shard_map.104 = (bf16[32,32,128]{2,1,0:T(8,128)(2,1)S(1)}, f32[1,128]{1,0:T(1,128)S(1)}) custom-call(s32[2,16]{1,0:T(2,128)S(1)} %copy-done.4, bf16[32,32,128]{2,1,0:T(8,128)(2,1)S(1)} %bitcast.9, f32[1,2048]{1,0:T(1,128)S(1)} %bitcast.10, f32[1,2048]{1,0:T(1,128)S(1)} %bitcast.11, s32[16,16]{1,0:T(8,128)S(1)} %bitcast.12, s32[16,16]{1,0:T(8,128)S(1)} %copy-done.3, ...), custom_call_target="tpu_custom_call" | custom-call | tf_op jit(solution)/shard_map/pallas_call | solution.py:419
  49.5 0.8 %reshape.31 = bf16[2,16,4096]{2,1,0:T(8,128)(2,1)} reshape(bf16[32,32,128]{2,1,0:T(8,128)(2,1)S(1)} %get-tuple-element.4) | data formatting | bytes 524288 | tf_op jit(solution)/shard_map/reshape | solution.py:473
  50.3 0.6 %reshape_squeeze.3 = f32[2,16]{1,0:T(2,128)} reshape(f32[32]{0:T(128)S(1)} %slice_reduce_fusion) | data formatting | bytes 256 | tf_op jit(solution)/shard_map/reshape;squeeze | solution.py:474
  (1 shorter events, 0.0 us)
Async XLA Ops:
  1.6 0.7 %copy-start = (f32[2048]{0:T(1024)S(1)}, f32[2048]{0:T(1024)}, u32[]{:S(2)}) copy-start(f32[2048]{0:T(1024)} %param.10) | copy-start | bytes 24580
  2.3 0.7 %copy-start.1 = (f32[2048]{0:T(1024)S(1)}, f32[2048]{0:T(1024)}, u32[]{:S(2)}) copy-start(f32[2048]{0:T(1024)} %param.11) | copy-start | bytes 24580
  3.0 0.7 %copy-start.2 = (s32[16,16,1]{1,2,0:T(1,128)S(1)}, s32[16,16,1]{1,2,0:T(1,128)}, u32[]{:S(2)}) copy-start(s32[16,16,1]{1,2,0:T(1,128)} %param.16) | copy-start | bytes 3076
  3.7 0.7 %copy-start.3 = (s32[16,16]{1,0:T(8,128)S(1)}, s32[16,16]{1,0:T(8,128)}, u32[]{:S(2)}) copy-start(s32[16,16]{1,0:T(8,128)} %lengths.1) | copy-start | bytes 3076
  4.4 0.7 %copy-start.4 = (s32[2,16]{1,0:T(2,128)S(1)}, s32[2,16]{1,0:T(2,128)}, u32[]{:S(2)}) copy-start(s32[2,16]{1,0:T(2,128)} %bounds_smem.1) | copy-start | bytes 388

commit v6 on v5

--- a/solution.py
+++ b/solution.py
@@ -297,8 +297,6 @@
                 packed = jnp.where(stat_col == stat_row + 2 * heads, largest, packed)
                 stats[peer, slot : slot + 1, :] = jnp.sum(packed, axis=0, keepdims=True)
 
-    serve(me, got_r, got_s)
-
     @pl.loop(1, n)
     def _(step):
         peer = lax.rem(me + n - offset(step), n)
@@ -306,6 +304,8 @@
         serve(peer, sent_r, sent_s)
         reply_copy(peer, me).start()
         stat_copy(peer, me).start()
+
+    serve(me, got_r, got_s)
 
     for chunk in range(chunks):
         load(2, chunk).wait()

time: 51.4 us -> 52.4 us (1.019)
  the two profiles are of different devices: /device:TPU:0 before, /device:TPU:17 now
where the time goes in v6:
time: 52.4 us; the launch traced here: 52 us
  Pallas kernels  45.5 us (87%)
  local copies, waits for them, and re-layouts  5.93 us (11%)
  between operations  0.66 us (1%)
    pallas_call x1, Pallas kernels, body(): pl.pallas_call(functools.partial(kernel, n, resident), out_shape=(jax.Sha...  45.5 us
    unnamed x11, local copies, waits for them, and re-layouts  4.45 us

profile of v6, /device:TPU:17, one launch (start us, length us, event | category | flops | bytes accessed | tf_op | source)
XLA Modules:
  0.0 52.0 jit_solution(14541038789753218228)
XLA Ops:
  0.6 1.0 %copy.11 = bf16[4,8,32,128]{3,2,1,0:T(8,128)(2,1)S(1)} copy(bf16[4,8,32,128]{3,1,2,0:T(8,128)(2,1)} %bitcast.16) | data formatting | bytes 524288
  1.6 0.0 copy-start
  1.6 0.7 %copy-done = f32[2048]{0:T(1024)S(1)} copy-done((f32[2048]{0:T(1024)S(1)}, f32[2048]{0:T(1024)}, u32[]{:S(2)}) %copy-start) | copy-done | bytes 8216
  2.3 0.0 copy-start.1
  2.3 0.7 %copy-done.1 = f32[2048]{0:T(1024)S(1)} copy-done((f32[2048]{0:T(1024)S(1)}, f32[2048]{0:T(1024)}, u32[]{:S(2)}) %copy-start.1) | copy-done | bytes 8216
  3.0 0.0 copy-start.2
  3.0 0.7 %copy-done.2 = s32[16,16,1]{1,2,0:T(1,128)S(1)} copy-done((s32[16,16,1]{1,2,0:T(1,128)S(1)}, s32[16,16,1]{1,2,0:T(1,128)}, u32[]{:S(2)}) %copy-start.2) | copy-done | bytes 1048
  3.7 0.0 copy-start.3
  3.7 0.7 %copy-done.3 = s32[16,16]{1,0:T(8,128)S(1)} copy-done((s32[16,16]{1,0:T(8,128)S(1)}, s32[16,16]{1,0:T(8,128)}, u32[]{:S(2)}) %copy-start.3) | copy-done | bytes 1048
  4.4 0.0 copy-start.4
  4.4 0.7 %copy-done.4 = s32[2,16]{1,0:T(2,128)S(1)} copy-done((s32[2,16]{1,0:T(2,128)S(1)}, s32[2,16]{1,0:T(2,128)}, u32[]{:S(2)}) %copy-start.4) | copy-done | bytes 152
  5.1 45.5 %shard_map.104 = (bf16[32,32,128]{2,1,0:T(8,128)(2,1)S(1)}, f32[1,128]{1,0:T(1,128)S(1)}) custom-call(s32[2,16]{1,0:T(2,128)S(1)} %copy-done.4, bf16[32,32,128]{2,1,0:T(8,128)(2,1)S(1)} %bitcast.9, f32[1,2048]{1,0:T(1,128)S(1)} %bitcast.10, f32[1,2048]{1,0:T(1,128)S(1)} %bitcast.11, s32[16,16]{1,0:T(8,128)S(1)} %bitcast.12, s32[16,16]{1,0:T(8,128)S(1)} %copy-done.3, ...), custom_call_target="tpu_custom_call" | custom-call | tf_op jit(solution)/shard_map/pallas_call | solution.py:419
  50.6 0.8 %reshape.31 = bf16[2,16,4096]{2,1,0:T(8,128)(2,1)} reshape(bf16[32,32,128]{2,1,0:T(8,128)(2,1)S(1)} %get-tuple-element.4) | data formatting | bytes 524288 | tf_op jit(solution)/shard_map/reshape | solution.py:473
  51.4 0.6 %reshape_squeeze.3 = f32[2,16]{1,0:T(2,128)} reshape(f32[32]{0:T(128)S(1)} %slice_reduce_fusion) | data formatting | bytes 256 | tf_op jit(solution)/shard_map/reshape;squeeze | solution.py:474
  (1 shorter events, 0.0 us)
Async XLA Ops:
  1.6 0.7 %copy-start = (f32[2048]{0:T(1024)S(1)}, f32[2048]{0:T(1024)}, u32[]{:S(2)}) copy-start(f32[2048]{0:T(1024)} %param.10) | copy-start | bytes 24580
  2.3 0.7 %copy-start.1 = (f32[2048]{0:T(1024)S(1)}, f32[2048]{0:T(1024)}, u32[]{:S(2)}) copy-start(f32[2048]{0:T(1024)} %param.11) | copy-start | bytes 24580
  3.0 0.7 %copy-start.2 = (s32[16,16,1]{1,2,0:T(1,128)S(1)}, s32[16,16,1]{1,2,0:T(1,128)}, u32[]{:S(2)}) copy-start(s32[16,16,1]{1,2,0:T(1,128)} %param.16) | copy-start | bytes 3076
  3.7 0.7 %copy-start.3 = (s32[16,16]{1,0:T(8,128)S(1)}, s32[16,16]{1,0:T(8,128)}, u32[]{:S(2)}) copy-start(s32[16,16]{1,0:T(8,128)} %lengths.1) | copy-start | bytes 3076
  4.4 0.7 %copy-start.4 = (s32[2,16]{1,0:T(2,128)S(1)}, s32[2,16]{1,0:T(2,128)}, u32[]{:S(2)}) copy-start(s32[2,16]{1,0:T(2,128)} %bounds_smem.1) | copy-start | bytes 388
